TPU v7x, 32 devices: a whole 2x2x4 slice. The times are simulated.
32 devices in a mesh: dp: 8 (over z, y), expert: 4 (over x, core).
Axes of the slice: x: 2, y: 2, z: 4, core: 2. Of those that a mesh axis runs over, the one named last changes fastest.
Arguments:
- master: float32 [4, 4096, 1536], P('expert', 'dp'), may hold values from -0.109375 to 0.109375
- moment_one: float32 [4, 4096, 1536], P('expert', 'dp'), may hold values from -1.5 to 1.5
- moment_two: float32 [4, 4096, 1536], P('expert', 'dp'), may hold values from 0.0001 to 0.003
- saved_rows: bfloat16 [4, 3072, 1536], P('expert', 'dp'), may hold values from -6 to 6
- saved_grads: bfloat16 [4, 3072, 4096], P('expert', 'dp'), may hold values from -0.15625 to 0.15625
- slot_rows: bfloat16 [4096, 2, 1536], P(('dp', 'expert')), may hold values from -6 to 6
- routes: int32 [4096, 2], P(('dp', 'expert')), may hold values from 0 to 3, all different within a row; in each aligned block of 128 rows (0 to 127, 128 to 255, ...) at most 80 rows name the same one
- gates: float32 [4096, 2], P(('dp', 'expert')), may hold values from 0.1 to 1
Outputs:
- master_new: float32 [4, 4096, 1536], P('expert', 'dp')
- moment_one_new: float32 [4, 4096, 1536], P('expert', 'dp')
- moment_two_new: float32 [4, 4096, 1536], P('expert', 'dp')
- mixed: bfloat16 [4096, 4096], P(('dp', 'expert'))
Inputs may be any that keep to these rules, and one draw needn't show every extreme that they name: `routes`: each token names 2 different experts. Among the 128 tokens of one device (aligned blocks of rows in device order, dp slowest) at most 80 name the same expert, and in some device's block exactly 80 do.
All inputs are finite; a program needn't handle non-finite values.
Results may differ from a plain program's by a relative error of at most 0.034.
Values may be sent and summed in bfloat16 or wider, within the bound.
A program may use at most 128 MiB of HBM per device.

v0:
```python
import jax
import jax.numpy as jnp
from jax import lax
from jax.sharding import PartitionSpec as P

beta_one = 0.9
beta_two = 0.999
learn_rate = 0.002
tiny_eps = 1e-08
steps_done = 100.0


def adam_update(master, moment_one, moment_two, grad):
    m_new = beta_one * moment_one + (1.0 - beta_one) * grad
    v_new = beta_two * moment_two + (1.0 - beta_two) * grad * grad
    fix_one = 1.0 - beta_one**steps_done
    fix_two = 1.0 - beta_two**steps_done
    step_size = m_new / fix_one / (jnp.sqrt(v_new / fix_two) + tiny_eps)
    return (master - learn_rate * step_size, m_new, v_new)


def slot_places(routes, experts):
    flat = routes.reshape(-1)
    onehot = (flat[:, None] == jnp.arange(experts, dtype=jnp.int32)[None, :]).astype(jnp.int32)
    place = jnp.sum((jnp.cumsum(onehot, axis=0) - onehot) * onehot, axis=1)
    return (flat, place)


def send_back(results):
    return lax.all_to_all(results, "expert", split_axis=0, concat_axis=0, tiled=True)


def body(master, moment_one, moment_two, saved_rows, saved_grads, slot_rows, routes, gates):
    rows_here = saved_rows[0]
    grads_here = saved_grads[0]
    grad = lax.psum_scatter(
        lax.dot_general(
            grads_here, rows_here, (((0,), (0,)), ((), ())), preferred_element_type=jnp.float32
        ).astype(jnp.bfloat16),
        "dp",
        scatter_dimension=0,
        tiled=True,
    ).astype(jnp.float32)
    master_new, m_new, v_new = adam_update(master[0], moment_one[0], moment_two[0], grad)
    weights_shard = master_new.astype(jnp.bfloat16)
    experts = lax.axis_size("expert")
    tok_count, top_count, width = slot_rows.shape
    capacity = tok_count * top_count * 5 // (4 * experts)
    flat, place = slot_places(routes, experts)
    outgoing = (
        jnp.zeros((experts, capacity, width), jnp.bfloat16)
        .at[flat, place]
        .set(slot_rows.reshape(-1, width))
    )
    weights = lax.all_gather(weights_shard, "dp", axis=0, tiled=True)
    out_width = weights.shape[0]
    received = lax.all_to_all(outgoing, "expert", split_axis=0, concat_axis=0, tiled=True)
    sources, count, _ = received.shape
    product = lax.dot_general(
        received.reshape(-1, width),
        weights,
        (((1,), (1,)), ((), ())),
        preferred_element_type=jnp.float32,
    )
    returned = send_back(product.astype(jnp.bfloat16).reshape(sources, count, out_width))
    out_width = returned.shape[2]
    picked = returned[flat, place].astype(jnp.float32).reshape(tok_count, top_count, out_width)
    mixed = jnp.sum(picked * gates[:, :, None], axis=1).astype(jnp.bfloat16)
    return (master_new[None], m_new[None], v_new[None], mixed)


def solution(mesh):
    placed = (
        P("expert", "dp", None),
        P("expert", "dp", None),
        P("expert", "dp", None),
        P("expert", "dp", None),
        P("expert", "dp", None),
        P(("dp", "expert"), None, None),
        P(("dp", "expert"), None),
        P(("dp", "expert"), None),
    )
    return jax.shard_map(
        body,
        mesh=mesh,
        in_specs=placed,
        out_specs=(
            P("expert", "dp", None),
            P("expert", "dp", None),
            P("expert", "dp", None),
            P(("dp", "expert"), None),
        ),
        check_vma=False,
    )
```

profile of v0, /device:TPU:0, one launch (start us, length us, event | category | flops | bytes accessed | tf_op | source)
XLA Modules:
  0.0 494.2 jit_solution(17850885533270439711)
XLA Ops:
  7.2 0.0 copy-start
  7.2 0.0 reduce-scatter.2.cloned.1.call-start
  7.2 1.8 copy-done
  9.1 10.9 %convolution_convert_fusion = bf16[4096,1536]{1,0:T(8,128)(2,1)} fusion(bf16[1,384,4096]{2,1,0:T(8,128)(2,1)S(1)} %copy-done, bf16[1,384,1536]{2,1,0:T(8,128)(2,1)} %param.11), kind=kOutput, calls=%fused_computation.2 | convolution fusion | flops 4838129664 | bytes 16908288 | tf_op jit(solution)/shard_map/dot_general | solution.py:37
  20.0 0.0 copy-start.2
  20.0 0.0 reduce-scatter.2.cloned.1.call-update
  20.0 0.0 copy-start.3
  20.0 0.0 all-gather.2.cloned.1.call-start
  20.1 210.1 %reduce-scatter.2.cloned.1.call-done = bf16[512,1536]{1,0:T(8,128)(2,1)} async-done(((bf16[4096,1536]{1,0:T(8,128)(2,1)}), bf16[512,1536]{1,0:T(8,128)(2,1)}) %reduce-scatter.2.cloned.1.call-update) | async-done | bytes 1572880 | tf_op jit(solution)/shard_map/reduce_scatter | solution.py:36
  230.1 0.0 copy-done.2
  230.1 8.5 %fusion.10 = (bf16[512,1536]{1,0:T(8,128)(2,1)}, f32[512,1536]{1,0:T(8,128)}, f32[1,512,1536]{2,1,0:T(8,128)}, f32[1,512,1536]{2,1,0:T(8,128)}) fusion(f32[1,512,1536]{2,1,0:T(8,128)S(1)} %copy-done.2, bf16[512,1536]{1,0:T(8,128)(2,1)} %reduce-scatter.2.cloned.1.call-done, f32[1,512,1536]{2,1,0:T(8,128)} %param.9, f32[1,512,1536]{2,1,0:T(8,128)} %param.8), kind=kLoop, calls=%fused_computation.27 | loop fusion | flops 11796480 | bytes 22020096 | tf_op jit(solution)/shard_map/convert_element_type | solution.py:45
  238.7 0.0 all-gather.2.cloned.1.call-update
  238.7 0.0 copy-done.3
  238.7 0.1 copy.15
  238.8 0.1 reshape.87
  238.9 0.1 eq.29
  239.1 0.1 eq.25
  239.2 1.2 reduce-window.6
  240.5 0.1 slice.12
  240.5 0.1 copy.18
  240.7 0.1 copy.19
  240.8 2.3 reshape.101
  243.1 0.1 add_bitcast_fusion
  243.2 0.1 broadcast_in_dim.21
  243.2 19.8 %scatter_fusion = bf16[4,80,1536]{2,1,0:T(8,128)(2,1)S(1)} fusion(bf16[4,80,1536]{2,1,0:T(8,128)(2,1)S(1)} %broadcast_in_dim.21, s32[256]{0:T(256)S(1)} %bitcast.55, bf16[256,1536]{1,0:T(8,128)(2,1)S(1)} %reshape.101), kind=kCustom, calls=%fused_computation.1 | custom fusion | bytes 2361344 | tf_op jit(solution)/shard_map/scatter | solution.py:53
  263.0 16.3 %all_to_all.10 = bf16[4,80,1536]{2,1,0:T(8,128)(2,1)S(1)} all-to-all(bf16[4,80,1536]{2,1,0:T(8,128)(2,1)S(1)} %scatter_fusion), channel_id=1, replica_groups=mesh['dp'=8,'expert'=4] {'expert'}, dimensions={0} | all-to-all | bytes 1966080 | tf_op jit(solution)/shard_map/all_to_all | solution.py:57
  279.3 135.1 %all-gather.2.cloned.1.call-done = bf16[4096,1536]{1,0:T(8,128)(2,1)} async-done(((bf16[512,1536]{1,0:T(8,128)(2,1)}), bf16[4096,1536]{1,0:T(8,128)(2,1)}) %all-gather.2.cloned.1.call-update) | async-done | bytes 12582928 | tf_op jit(solution)/shard_map/all_gather | solution.py:55
  414.4 14.1 %convolution_convert_fusion.1 = bf16[320,4096]{1,0:T(8,128)(2,1)} fusion(bf16[320,1536]{1,0:T(8,128)(2,1)S(1)} %bitcast.58, bf16[4096,1536]{1,0:T(8,128)(2,1)} %all-gather.2.cloned.1.call-done), kind=kOutput, calls=%fused_computation.3 | convolution fusion | flops 4027842560 | bytes 16187392 | tf_op jit(solution)/shard_map/dot_general | solution.py:59
  428.5 0.0 copy-start.4
  428.5 4.0 all-to-all-start.1
  432.4 0.0 copy-done.4
  432.4 0.1 copy.20
  432.6 31.0 %all-to-all-done.1 = bf16[4,80,4096]{2,1,0:T(8,128)(2,1)S(1)} async-done(((bf16[4,80,4096]{2,1,0:T(8,128)(2,1)}), bf16[4,80,4096]{2,1,0:T(8,128)(2,1)S(1)}, u32[]{:S(2)}, u32[]{:S(2)}) %all-to-all-start.1) | async-done | bytes 2621472 | tf_op jit(solution)/shard_map/all_to_all | solution.py:30
  463.5 8.5 %gather_fusion = bf16[256,4096]{1,0:T(8,128)(2,1)} fusion(bf16[4,80,4096]{2,1,0:T(8,128)(2,1)S(1)} %all-to-all-done.1, s32[256]{0:T(256)S(1)} %bitcast.54), kind=kCustom, calls=%fused_computation | custom fusion | bytes 4196352 | tf_op jit(solution)/shard_map/gather | solution.py:67
  472.1 0.0 copy-start.1
  472.1 5.6 %reshape.92 = f32[128,2,4096]{2,1,0:T(2,128)} reshape(bf16[256,4096]{1,0:T(8,128)(2,1)} %gather_fusion) | data formatting | bytes 6291456 | tf_op jit(solution)/shard_map/convert_element_type | solution.py:67
  477.7 9.6 %multiply_reduce_fusion = bf16[128,4096]{1,0:T(8,128)(2,1)} fusion(f32[128,2,4096]{2,1,0:T(2,128)} %reshape.92, f32[128,2]{1,0:T(8,128)S(1)} %copy.20), kind=kLoop, calls=%fused_computation.5 | loop fusion | flops 1572864 | bytes 5243904 | tf_op jit(solution)/shard_map/reduce_sum | solution.py:68
  487.3 0.0 copy-done.1
  (5 shorter events, 0.1 us)
Async XLA Ops:
  7.2 1.9 copy-start
  7.2 223.0 %reduce-scatter.2.cloned.1.call-start = ((), (), s32[]{:S(2)}) async-start(), calls=%async_computation.3 | async-start | bytes 14155776 | tf_op jit(solution)/shard_map/reduce_scatter | solution.py:36
  20.0 210.2 %copy-start.2 = (f32[1,512,1536]{2,1,0:T(8,128)S(1)}, f32[1,512,1536]{2,1,0:T(8,128)}, u32[]{:S(2)}) copy-start(f32[1,512,1536]{2,1,0:T(8,128)} %param.10) | copy-start | bytes 9437188
  20.0 218.7 %copy-start.3 = (s32[128,2]{0,1:T(2,128)S(1)}, s32[128,2]{0,1:T(2,128)}, u32[]{:S(2)}) copy-start(s32[128,2]{0,1:T(2,128)} %param.14) | copy-start | bytes 3076
  20.0 394.4 %all-gather.2.cloned.1.call-start = ((), (), s32[]{:S(2)}) async-start(), calls=%async_computation.4 | async-start | bytes 14155776 | tf_op jit(solution)/shard_map/all_gather | solution.py:55
  428.5 4.0 copy-start.4
  428.5 35.1 %all-to-all-start.1 = ((bf16[4,80,4096]{2,1,0:T(8,128)(2,1)}), bf16[4,80,4096]{2,1,0:T(8,128)(2,1)S(1)}, u32[]{:S(2)}, u32[]{:S(2)}) async-start(bf16[4,80,4096]{2,1,0:T(8,128)(2,1)} %bitcast.57), calls=%async_computation.2 | async-start | bytes 5242880 | tf_op jit(solution)/shard_map/all_to_all | solution.py:30
  472.1 15.2 %copy-start.1 = (bf16[1,384,4096]{2,1,0:T(8,128)(2,1)S(1)}, bf16[1,384,4096]{2,1,0:T(8,128)(2,1)}, u32[]{:S(2)}) copy-start(bf16[1,384,4096]{2,1,0:T(8,128)(2,1)} %param.12) | copy-start | bytes 9437188
Sparse Core Ops, SparseCore 0:
  20.1 209.9 reduce-scatter.1
  238.8 175.5 all-gather.1
where the time goes:
time: 495 us; the launch traced here: 494 us
  waiting for transfers between devices  376 us (76%)
  local copies, waits for them, and re-layouts  39 us (8%)
  matrix products  25 us (5%)
  other arithmetic  19.5 us (4%)
  blocking collectives  16.3 us (3%)
  between operations  14.1 us (3%)
    reduce_scatter x1, waiting for transfers between devices, body(): lax.psum_scatter(lax.dot_general(grads_here, rows_here, (((0,), (0,)), ((...  210 us
    all_gather x1, waiting for transfers between devices, body(): weights = lax.all_gather(weights_shard, 'dp', axis=0, tiled=True)  135 us
    all_to_all x1, waiting for transfers between devices, send_back(): lax.all_to_all(results, 'expert', split_axis=0, concat_axis=0, tiled=True)  31 us
    scatter x1, local copies, waits for them, and re-layouts, body(): outgoing = jnp.zeros((experts, capacity, width), jnp.bfloat16).at[flat, p...  19.8 us
    all_to_all x1, blocking collectives, body(): lax.all_to_all(outgoing, 'expert', split_axis=0, concat_axis=0, tiled=True)  16.3 us
    dot_general x1, matrix products, body(): lax.dot_general(received.reshape(-1, width), weights, (((1,), (1,)), ((),...  14.1 us
    dot_general x1, matrix products, body(): lax.dot_general(grads_here, rows_here, (((0,), (0,)), ((), ())), preferre...  10.9 us
  transfers between devices with their start and end apart: 3, of which 3 were waited for; matrix products, arithmetic and copies ran while one was open for 5% of the time, Pallas kernels for 0%

commit v1 on v0

v1 whole, which is shorter than its diff:
```python
import functools

import jax
import jax.numpy as jnp
from jax import lax
from jax.experimental import pallas as pl
from jax.experimental.pallas import tpu as pltpu
from jax.sharding import PartitionSpec as P

beta_one = 0.9
beta_two = 0.999
learn_rate = 0.002
tiny_eps = 1e-08
steps_done = 100.0

MESH = pl.DeviceIdType.MESH


def adam_update(master, moment_one, moment_two, grad):
    m_new = beta_one * moment_one + (1.0 - beta_one) * grad
    v_new = beta_two * moment_two + (1.0 - beta_two) * grad * grad
    fix_one = 1.0 - beta_one**steps_done
    fix_two = 1.0 - beta_two**steps_done
    step_size = m_new / fix_one / (jnp.sqrt(v_new / fix_two) + tiny_eps)
    return (master - learn_rate * step_size, m_new, v_new)


def lanes_of(shard):
    if shard % 512 == 0:
        part = shard // 4
        return ((1, 0, part), (-1, part, part), (1, 2 * part, part), (-1, 3 * part, part))
    return ((1, 0, shard),)


def ring_place(index, n):
    return jnp.where(lax.rem(index, 2) == 0, index // 2, (2 * n - 1 - index) // 2)


def ring_index(place, n):
    place = lax.rem(place + 2 * n, n)
    return jnp.where(place < n // 2, 2 * place, 2 * n - 1 - 2 * place)


def greet(n, experts, here, expert):
    barrier = pltpu.get_barrier_semaphore()
    for step in (1, -1):
        pl.semaphore_signal(
            barrier, inc=1, device_id={"dp": ring_index(here + step, n)}, device_id_type=MESH
        )
    for other in range(1, experts):
        pl.semaphore_signal(
            barrier,
            inc=1,
            device_id={"expert": lax.rem(expert + other, experts)},
            device_id_type=MESH,
        )
    pl.semaphore_wait(barrier, experts + 1)


def reduce_kernel(
    n, experts, shard,
    rows_ref, grads_ref, out_ref, total_ref, got_ref,
    first, slots, part, send_sem, recv_sem, tok_send, tok_recv, own_sem,
):
    here = ring_place(lax.axis_index("dp"), n)
    expert = lax.axis_index("expert")
    lanes = lanes_of(shard)

    def partial(place, low, size):
        at = pl.multiple_of(ring_index(place, n) * shard + low, size)
        return lax.dot_general(
            grads_ref[:, pl.ds(at, size)],
            rows_ref[...],
            (((0,), (0,)), ((), ())),
            preferred_element_type=jnp.float32,
        )

    def send(step, lane, source):
        way, low, size = lanes[lane]
        return pltpu.make_async_remote_copy(
            src_ref=source.at[pl.ds(low, size)],
            dst_ref=slots.at[step, pl.ds(low, size)],
            send_sem=send_sem.at[step, lane],
            recv_sem=recv_sem.at[step, lane],
            device_id={"dp": ring_index(here + way, n)},
            device_id_type=MESH,
        )

    def token_copy(other):
        peer = lax.rem(expert + other, experts)
        return pltpu.make_async_remote_copy(
            src_ref=out_ref.at[peer],
            dst_ref=got_ref.at[expert],
            send_sem=tok_send.at[other],
            recv_sem=tok_recv.at[other],
            device_id={"expert": peer},
            device_id_type=MESH,
        )

    greet(n, experts, here, expert)
    for lane, (way, low, size) in enumerate(lanes):
        first[pl.ds(low, size)] = partial(here - way, low, size).astype(jnp.bfloat16)
        send(0, lane, first).start()
    for other in range(1, experts):
        token_copy(other).start()
    own = pltpu.make_async_copy(out_ref.at[expert], got_ref.at[expert], own_sem)
    own.start()

    def step_on(step, _):
        for lane, (way, low, size) in enumerate(lanes):
            part[pl.ds(low, size)] = partial(here - way * (2 + step), low, size)
            send(step, lane, first).wait_recv()
            slots[step, pl.ds(low, size)] = (
                slots[step, pl.ds(low, size)].astype(jnp.float32) + part[pl.ds(low, size)]
            ).astype(jnp.bfloat16)
            send(step + 1, lane, slots.at[step]).start()
        return 0

    lax.fori_loop(0, n - 2, step_on, 0)
    last = n - 2
    for lane, (way, low, size) in enumerate(lanes):
        part[pl.ds(low, size)] = partial(here, low, size)
    for lane, (way, low, size) in enumerate(lanes):
        send(last, lane, first).wait_recv()
        total_ref[pl.ds(low, size)] = (
            slots[last, pl.ds(low, size)].astype(jnp.float32) + part[pl.ds(low, size)]
        )

    def drain(step, _):
        for lane in range(len(lanes)):
            send(step, lane, first).wait_send()
        return 0

    lax.fori_loop(0, n - 1, drain, 0)
    for other in range(1, experts):
        token_copy(other).wait()
    own.wait()


def reduce_grad(n, experts, rows, grads, outgoing):
    saved, width = rows.shape
    depth = grads.shape[1]
    shard = depth // n
    lanes = len(lanes_of(shard))
    return pl.pallas_call(
        functools.partial(reduce_kernel, n, experts, shard),
        out_shape=(
            jax.ShapeDtypeStruct((shard, width), jnp.float32),
            jax.ShapeDtypeStruct(outgoing.shape, jnp.bfloat16),
        ),
        in_specs=[pl.BlockSpec(memory_space=pltpu.VMEM)] * 3,
        out_specs=(pl.BlockSpec(memory_space=pltpu.VMEM),) * 2,
        scratch_shapes=[
            pltpu.VMEM((shard, width), jnp.bfloat16),
            pltpu.VMEM((n - 1, shard, width), jnp.bfloat16),
            pltpu.VMEM((shard, width), jnp.float32),
            pltpu.SemaphoreType.DMA((n - 1, lanes)),
            pltpu.SemaphoreType.DMA((n - 1, lanes)),
            pltpu.SemaphoreType.DMA((experts,)),
            pltpu.SemaphoreType.DMA((experts,)),
            pltpu.SemaphoreType.DMA,
        ],
        compiler_params=pltpu.CompilerParams(
            collective_id=0, has_side_effects=True, vmem_limit_bytes=48 * 2**20
        ),
        cost_estimate=pl.CostEstimate(
            flops=2 * saved * width * depth, bytes_accessed=4 * depth * width, transcendentals=0
        ),
        name="reduce_grad",
    )(rows, grads, outgoing)


def product_kernel(
    n, experts, shard,
    weight_ref, tok_ref, back_ref,
    held, prod, send_sem, recv_sem, back_send, back_recv, own_sem,
):
    here = ring_place(lax.axis_index("dp"), n)
    expert = lax.axis_index("expert")
    lanes = lanes_of(shard)
    count = tok_ref.shape[0] // experts
    width = tok_ref.shape[1]

    def send(step, lane, source):
        way, low, size = lanes[lane]
        return pltpu.make_async_remote_copy(
            src_ref=source.at[pl.ds(low, size)],
            dst_ref=held.at[step, pl.ds(low, size)],
            send_sem=send_sem.at[step, lane],
            recv_sem=recv_sem.at[step, lane],
            device_id={"dp": ring_index(here + way, n)},
            device_id_type=MESH,
        )

    def back_copy(other, columns):
        peer = lax.rem(expert + other, experts)
        return pltpu.make_async_remote_copy(
            src_ref=prod.at[peer, :, columns],
            dst_ref=back_ref.at[expert, :, columns],
            send_sem=back_send.at[other],
            recv_sem=back_recv.at[other],
            device_id={"expert": peer},
            device_id_type=MESH,
        )

    def multiply(block, place, low, size):
        at = pl.multiple_of(ring_index(place, n) * shard + low, size)
        columns = pl.ds(at, size)
        out = lax.dot_general(
            tok_ref[...], block, (((1,), (1,)), ((), ())), preferred_element_type=jnp.float32
        )
        prod[:, :, columns] = out.astype(jnp.bfloat16).reshape(experts, count, size)
        for other in range(1, experts):
            back_copy(other, columns).start()
        pltpu.make_async_copy(
            prod.at[expert, :, columns], back_ref.at[expert, :, columns], own_sem
        ).start()

    greet(n, experts, here, expert)
    for lane in range(len(lanes)):
        send(0, lane, weight_ref).start()
    for way, low, size in lanes:
        multiply(weight_ref[pl.ds(low, size)], here, low, size)

    def step_on(step, _):
        for lane, (way, low, size) in enumerate(lanes):
            send(step, lane, weight_ref).wait_recv()

            @pl.when(step < n - 2)
            def _():
                send(step + 1, lane, held.at[step]).start()

            multiply(held[step, pl.ds(low, size)], here - way * (1 + step), low, size)
        return 0

    lax.fori_loop(0, n - 1, step_on, 0)

    def drain(step, _):
        for lane in range(len(lanes)):
            send(step, lane, weight_ref).wait_send()
        return 0

    lax.fori_loop(0, n - 1, drain, 0)
    for other in range(1, experts):
        back_copy(other, pl.ds(0, prod.shape[2])).wait()
    pltpu.make_async_copy(prod.at[expert], back_ref.at[expert], own_sem).wait()


def expert_product(n, experts, weights, tokens):
    shard, width = weights.shape
    depth = shard * n
    rows = tokens.shape[0]
    lanes = len(lanes_of(shard))
    return pl.pallas_call(
        functools.partial(product_kernel, n, experts, shard),
        out_shape=jax.ShapeDtypeStruct((experts, rows // experts, depth), jnp.bfloat16),
        in_specs=[pl.BlockSpec(memory_space=pltpu.VMEM)] * 2,
        out_specs=pl.BlockSpec(memory_space=pltpu.VMEM),
        scratch_shapes=[
            pltpu.VMEM((n - 1, shard, width), jnp.bfloat16),
            pltpu.VMEM((experts, rows // experts, depth), jnp.bfloat16),
            pltpu.SemaphoreType.DMA((n - 1, lanes)),
            pltpu.SemaphoreType.DMA((n - 1, lanes)),
            pltpu.SemaphoreType.DMA((experts,)),
            pltpu.SemaphoreType.DMA((experts,)),
            pltpu.SemaphoreType.DMA,
        ],
        compiler_params=pltpu.CompilerParams(
            collective_id=1, has_side_effects=True, vmem_limit_bytes=48 * 2**20
        ),
        cost_estimate=pl.CostEstimate(
            flops=2 * rows * width * depth, bytes_accessed=4 * depth * width, transcendentals=0
        ),
        name="expert_product",
    )(weights, tokens)


def body(n, master, moment_one, moment_two, saved_rows, saved_grads, slot_rows, routes, gates):
    experts = lax.axis_size("expert")
    tok_count, top_count, width = slot_rows.shape
    capacity = tok_count * top_count * 5 // (4 * experts)
    capacity = -(-capacity // 16) * 16
    flat = routes.reshape(-1)
    turn = jnp.arange(flat.shape[0], dtype=jnp.int32)
    same = (flat[:, None] == flat[None, :]) & (turn[None, :] < turn[:, None])
    slot = flat * capacity + jnp.sum(same.astype(jnp.int32), axis=1)
    places = jnp.arange(experts * capacity, dtype=jnp.int32)
    pick = (places[:, None] == slot[None, :]).astype(jnp.bfloat16)
    outgoing = (
        jnp.dot(pick, slot_rows.reshape(-1, width), preferred_element_type=jnp.float32)
        .astype(jnp.bfloat16)
        .reshape(experts, capacity, width)
    )
    grad, received = reduce_grad(n, experts, saved_rows[0], saved_grads[0], outgoing)
    master_new, m_new, v_new = adam_update(master[0], moment_one[0], moment_two[0], grad)
    returned = expert_product(
        n, experts, master_new.astype(jnp.bfloat16), received.reshape(-1, width)
    ).reshape(experts * capacity, -1)
    slot = slot.reshape(tok_count, top_count)
    share = jnp.sum(
        jnp.where(slot[:, :, None] == places[None, None, :], gates[:, :, None], 0.0), axis=1
    )
    high = share.astype(jnp.bfloat16)
    low = (share - high.astype(jnp.float32)).astype(jnp.bfloat16)
    mixed = jnp.dot(high, returned, preferred_element_type=jnp.float32) + jnp.dot(
        low, returned, preferred_element_type=jnp.float32
    )
    return (master_new[None], m_new[None], v_new[None], mixed.astype(jnp.bfloat16))


def solution(mesh):
    placed = (
        P("expert", "dp", None),
        P("expert", "dp", None),
        P("expert", "dp", None),
        P("expert", "dp", None),
        P("expert", "dp", None),
        P(("dp", "expert"), None, None),
        P(("dp", "expert"), None),
        P(("dp", "expert"), None),
    )
    return jax.shard_map(
        functools.partial(body, mesh.shape["dp"]),
        mesh=mesh,
        in_specs=placed,
        out_specs=(
            P("expert", "dp", None),
            P("expert", "dp", None),
            P("expert", "dp", None),
            P(("dp", "expert"), None),
        ),
        check_vma=False,
    )
```

time: 495 us -> 269 us (0.54)
  waiting for transfers between devices: 376 us -> 0 us
  Pallas kernels: 0 us -> 255 us
  local copies, waits for them, and re-layouts: 39 us -> 3.51 us
  matrix products: 25 us -> 2.9 us
  blocking collectives: 16.3 us -> 0 us
  between operations: 14.1 us -> 0.74 us
  other arithmetic: 19.5 us -> 7.45 us
    pallas_call x0 -> x2, Pallas kernels: none -> 255 us  [the longest x1 129 us: reduce_grad(): pl.pallas_call(functools.partial(reduce_kernel, n, experts, shard), out_s...]
    reduce_scatter x1 -> x0, waiting for transfers between devices: 210 us -> none  [body(): lax.psum_scatter(lax.dot_general(grads_here, rows_here, (((0,), (0,)), ((...]
    all_gather x1 -> x0, waiting for transfers between devices: 135 us -> none  [body(): weights = lax.all_gather(weights_shard, 'dp', axis=0, tiled=True)]
    all_to_all x1 -> x0, waiting for transfers between devices: 31 us -> none  [send_back(): lax.all_to_all(results, 'expert', split_axis=0, concat_axis=0, tiled=True)]
    dot_general x2 -> x3, matrix products: 25 us -> 2.9 us  [the longest x1 1.73 us: body(): jnp.dot(low, returned, preferred_element_type=jnp.float32)]
    scatter x1 -> x0, local copies, waits for them, and re-layouts: 19.8 us -> none  [body(): outgoing = jnp.zeros((experts, capacity, width), jnp.bfloat16).at[flat, p...]
    all_to_all x1 -> x0, blocking collectives: 16.3 us -> none  [body(): lax.all_to_all(outgoing, 'expert', split_axis=0, concat_axis=0, tiled=True)]
    reduce_sum x2, other arithmetic: 9.66 us -> 0.92 us  [the longest x1 0.73 us: body(): jnp.sum(jnp.where(slot[:, :, None] == places[None, None, :], gates[:, :,...]
  transfers between devices with their start and end apart: 3 -> 0, of which waited for: 3 -> 0; matrix products, arithmetic and copies ran while one was open for 5% -> 0% of each run, Pallas kernels for 0% -> 0%
where the time goes in v1:
time: 269 us
  Pallas kernels  255 us (95%)
  other arithmetic  7.45 us (3%)
  local copies, waits for them, and re-layouts  3.51 us (1%)
  matrix products  2.9 us (1%)
    pallas_call x1, Pallas kernels, reduce_grad(): pl.pallas_call(functools.partial(reduce_kernel, n, experts, shard), out_s...  129 us
    pallas_call x1, Pallas kernels, expert_product(): pl.pallas_call(functools.partial(product_kernel, n, experts, shard), out_...  126 us
    convert_element_type x1, other arithmetic, body(): master_new.astype(jnp.bfloat16)  5.81 us

profile of v1, /device:TPU:0, one launch (start us, length us, event | category | flops | bytes accessed | tf_op | source)
XLA Modules:
  0.0 269.2 jit_solution(709722066661216049)
XLA Ops:
  0.6 0.0 copy-start
  0.6 0.9 copy.22
  1.5 0.1 reshape.44
  1.7 0.2 convert_reduce_fusion
  1.9 0.1 reduce_sum.21
  2.0 0.1 copy.23
  2.1 0.7 multiply_add_fusion
  2.8 0.7 select_reduce_fusion
  3.5 2.3 reshape.45
  5.8 0.4 convolution_convert_fusion
  6.2 0.0 copy-done
  6.2 0.0 copy-start.1
  6.2 0.0 copy-start.2
  6.2 0.0 copy-start.3
  6.3 128.7 %reduce_grad.1 = (f32[512,1536]{1,0:T(8,128)}, bf16[4,80,1536]{2,1,0:T(8,128)(2,1)S(1)}) custom-call(bf16[384,1536]{1,0:T(8,128)(2,1)S(1)} %bitcast.33, bf16[384,4096]{1,0:T(8,128)(2,1)} %bitcast.36, bf16[4,80,1536]{2,1,0:T(8,128)(2,1)S(1)} %bitcast.32), custom_call_target="tpu_custom_call" | custom-call | flops 4831838208 | bytes 25165824 | tf_op jit(solution)/shard_map/reduce_grad/pallas_call | solution.py:145
  135.0 0.0 copy-done.1
  135.0 0.0 copy-done.2
  135.0 0.0 copy-done.3
  135.0 5.8 %fusion.9 = (bf16[512,1536]{1,0:T(8,128)(2,1)S(1)}, f32[512,1536]{1,0:T(8,128)}, f32[1,512,1536]{2,1,0:T(8,128)}, f32[1,512,1536]{2,1,0:T(8,128)}) fusion(f32[512,1536]{1,0:T(8,128)} %get-tuple-element.6, f32[1,512,1536]{2,1,0:T(8,128)S(1)} %copy-done.1, f32[1,512,1536]{2,1,0:T(8,128)S(1)} %copy-done.2, f32[1,512,1536]{2,1,0:T(8,128)S(1)} %copy-done.3), kind=kLoop, calls=%fused_computation.22 | loop fusion | flops 11010048 | bytes 23592960 | tf_op jit(solution)/shard_map/convert_element_type | solution.py:297
  140.8 125.8 %expert_product.1 = bf16[4,80,4096]{2,1,0:T(8,128)(2,1)S(1)} custom-call(bf16[512,1536]{1,0:T(8,128)(2,1)S(1)} %get-tuple-element.8.weight_ref, bf16[320,1536]{1,0:T(8,128)(2,1)S(1)} %bitcast.34), custom_call_target="tpu_custom_call" | custom-call | flops 4026531840 | bytes 25165824 | tf_op jit(solution)/shard_map/expert_product/pallas_call | solution.py:254
  266.7 0.7 fusion.7
  267.4 1.7 fusion
  (1 shorter events, 0.0 us)
Async XLA Ops:
  0.6 5.6 %copy-start = (bf16[1,384,1536]{2,1,0:T(8,128)(2,1)S(1)}, bf16[1,384,1536]{2,1,0:T(8,128)(2,1)}, u32[]{:S(2)}) copy-start(bf16[1,384,1536]{2,1,0:T(8,128)(2,1)} %param.11) | copy-start | bytes 3538948
  6.2 128.8 %copy-start.1 = (f32[1,512,1536]{2,1,0:T(8,128)S(1)}, f32[1,512,1536]{2,1,0:T(8,128)}, u32[]{:S(2)}) copy-start(f32[1,512,1536]{2,1,0:T(8,128)} %param.10) | copy-start | bytes 9437188
  6.2 128.8 %copy-start.2 = (f32[1,512,1536]{2,1,0:T(8,128)S(1)}, f32[1,512,1536]{2,1,0:T(8,128)}, u32[]{:S(2)}) copy-start(f32[1,512,1536]{2,1,0:T(8,128)} %param.9) | copy-start | bytes 9437188
  6.2 128.7 %copy-start.3 = (f32[1,512,1536]{2,1,0:T(8,128)S(1)}, f32[1,512,1536]{2,1,0:T(8,128)}, u32[]{:S(2)}) copy-start(f32[1,512,1536]{2,1,0:T(8,128)} %param.8) | copy-start | bytes 9437188

commit v2 on v1

--- a/solution.py
+++ b/solution.py
@@ -173,96 +173,178 @@
 def product_kernel(
     n, experts, shard,
     weight_ref, tok_ref, back_ref,
-    held, prod, send_sem, recv_sem, back_send, back_recv, own_sem,
+    mate, held, prod, send_sem, recv_sem, mate_sem, back_send, back_recv, own_sem,
 ):
-    here = ring_place(lax.axis_index("dp"), n)
+    index = lax.axis_index("dp")
     expert = lax.axis_index("expert")
-    lanes = lanes_of(shard)
+    place, column = index // 2, lax.rem(index, 2)
+    twin = place * 2 + 1 - column
+    length = n // 2
+    has_left = place > 0
+    has_right = place < length - 1
+    size = 128
+    parts = shard // size
     count = tok_ref.shape[0] // experts
-    width = tok_ref.shape[1]
-
-    def send(step, lane, source):
-        way, low, size = lanes[lane]
+    half = length * shard
+
+    def send(way, block, part, source):
         return pltpu.make_async_remote_copy(
-            src_ref=source.at[pl.ds(low, size)],
-            dst_ref=held.at[step, pl.ds(low, size)],
-            send_sem=send_sem.at[step, lane],
-            recv_sem=recv_sem.at[step, lane],
-            device_id={"dp": ring_index(here + way, n)},
-            device_id_type=MESH,
-        )
-
-    def back_copy(other, columns):
+            src_ref=source.at[pl.ds(part * size, size)],
+            dst_ref=held.at[block, pl.ds(part * size, size)],
+            send_sem=send_sem.at[(way + 1) // 2, block, part],
+            recv_sem=recv_sem.at[block, part],
+            device_id={"dp": jnp.clip(place + way, 0, length - 1) * 2 + column},
+            device_id_type=MESH,
+        )
+
+    def swap():
+        return pltpu.make_async_remote_copy(
+            src_ref=tok_ref,
+            dst_ref=mate,
+            send_sem=mate_sem.at[0],
+            recv_sem=mate_sem.at[1],
+            device_id={"dp": twin},
+            device_id_type=MESH,
+        )
+
+    def back_copy(side, other, here, there):
         peer = lax.rem(expert + other, experts)
         return pltpu.make_async_remote_copy(
-            src_ref=prod.at[peer, :, columns],
-            dst_ref=back_ref.at[expert, :, columns],
-            send_sem=back_send.at[other],
-            recv_sem=back_recv.at[other],
-            device_id={"expert": peer},
-            device_id_type=MESH,
-        )
-
-    def multiply(block, place, low, size):
-        at = pl.multiple_of(ring_index(place, n) * shard + low, size)
-        columns = pl.ds(at, size)
+            src_ref=prod.at[side, peer, :, here],
+            dst_ref=back_ref.at[expert, :, there],
+            send_sem=back_send.at[side, other],
+            recv_sem=back_recv.at[side, other],
+            device_id={"dp": twin if side else index, "expert": peer},
+            device_id_type=MESH,
+        )
+
+    def multiply(side, weights, block, part):
+        here = pl.ds(pl.multiple_of(block * shard + part * size, size), size)
+        there = pl.ds(
+            pl.multiple_of((block * 2 + column) * shard + part * size, size), size
+        )
         out = lax.dot_general(
-            tok_ref[...], block, (((1,), (1,)), ((), ())), preferred_element_type=jnp.float32
-        )
-        prod[:, :, columns] = out.astype(jnp.bfloat16).reshape(experts, count, size)
-        for other in range(1, experts):
-            back_copy(other, columns).start()
-        pltpu.make_async_copy(
-            prod.at[expert, :, columns], back_ref.at[expert, :, columns], own_sem
-        ).start()
-
-    greet(n, experts, here, expert)
-    for lane in range(len(lanes)):
-        send(0, lane, weight_ref).start()
-    for way, low, size in lanes:
-        multiply(weight_ref[pl.ds(low, size)], here, low, size)
+            (mate if side else tok_ref)[...],
+            weights,
+            (((1,), (1,)), ((), ())),
+            preferred_element_type=jnp.float32,
+        )
+        prod[side, :, :, here] = out.astype(jnp.bfloat16).reshape(experts, count, size)
+        for other in range(1 - side, experts):
+            back_copy(side, other, here, there).start()
+        if side == 0:
+            pltpu.make_async_copy(
+                prod.at[0, expert, :, here], back_ref.at[expert, :, there], own_sem
+            ).start()
+
+    barrier = pltpu.get_barrier_semaphore()
+    for way, there in ((-1, has_left), (1, has_right)):
+
+        @pl.when(there)
+        def _():
+            pl.semaphore_signal(
+                barrier,
+                inc=1,
+                device_id={"dp": jnp.clip(place + way, 0, length - 1) * 2 + column},
+                device_id_type=MESH,
+            )
+
+    for other in range(experts):
+        peer = lax.rem(expert + other, experts)
+        for to in (index, twin) if other else (twin,):
+            pl.semaphore_signal(
+                barrier, inc=1, device_id={"dp": to, "expert": peer}, device_id_type=MESH
+            )
+    pl.semaphore_wait(
+        barrier, 2 * experts - 1 + has_left.astype(jnp.int32) + has_right.astype(jnp.int32)
+    )
+
+    swap().start()
+    for part in range(parts):
+        for way, there in ((-1, has_left), (1, has_right)):
+
+            @pl.when(there)
+            def _():
+                send(way, place, part, weight_ref).start()
+
+    for part in range(parts):
+        multiply(0, weight_ref[pl.ds(part * size, size)], place, part)
+    swap().wait()
+    for part in range(parts):
+        multiply(1, weight_ref[pl.ds(part * size, size)], place, part)
+
+    def take(way, block, part, onward):
+        send(way, block, part, weight_ref).wait_recv()
+
+        @pl.when(onward)
+        def _():
+            send(way, block, part, held.at[block]).start()
+
+        weights = held[block, pl.ds(part * size, size)]
+        multiply(0, weights, block, part)
+        multiply(1, weights, block, part)
 
     def step_on(step, _):
-        for lane, (way, low, size) in enumerate(lanes):
-            send(step, lane, weight_ref).wait_recv()
-
-            @pl.when(step < n - 2)
+        for part in range(parts):
+            before = place - 1 - step
+
+            @pl.when(before >= 0)
             def _():
-                send(step + 1, lane, held.at[step]).start()
-
-            multiply(held[step, pl.ds(low, size)], here - way * (1 + step), low, size)
+                take(1, before, part, has_right)
+
+            after = place + 1 + step
+
+            @pl.when(after < length)
+            def _():
+                take(-1, after, part, has_left)
+
         return 0
 
-    lax.fori_loop(0, n - 1, step_on, 0)
-
-    def drain(step, _):
-        for lane in range(len(lanes)):
-            send(step, lane, weight_ref).wait_send()
+    lax.fori_loop(0, length - 1, step_on, 0)
+
+    def drain(block, _):
+        for part in range(parts):
+
+            @pl.when((block <= place) & has_right)
+            def _():
+                send(1, block, part, weight_ref).wait_send()
+
+            @pl.when((block >= place) & has_left)
+            def _():
+                send(-1, block, part, weight_ref).wait_send()
+
         return 0
 
-    lax.fori_loop(0, n - 1, drain, 0)
-    for other in range(1, experts):
-        back_copy(other, pl.ds(0, prod.shape[2])).wait()
-    pltpu.make_async_copy(prod.at[expert], back_ref.at[expert], own_sem).wait()
+    lax.fori_loop(0, length, drain, 0)
+    whole = pl.ds(0, half)
+    for side in (0, 1):
+        for other in range(1 - side, experts):
+            back_copy(side, other, whole, whole).wait()
+    pltpu.make_async_copy(
+        prod.at[0, expert], back_ref.at[expert, :, whole], own_sem
+    ).wait()
 
 
 def expert_product(n, experts, weights, tokens):
     shard, width = weights.shape
     depth = shard * n
     rows = tokens.shape[0]
-    lanes = len(lanes_of(shard))
+    count = rows // experts
+    parts = shard // 128
     return pl.pallas_call(
         functools.partial(product_kernel, n, experts, shard),
-        out_shape=jax.ShapeDtypeStruct((experts, rows // experts, depth), jnp.bfloat16),
+        out_shape=jax.ShapeDtypeStruct((experts, count, depth), jnp.bfloat16),
         in_specs=[pl.BlockSpec(memory_space=pltpu.VMEM)] * 2,
         out_specs=pl.BlockSpec(memory_space=pltpu.VMEM),
         scratch_shapes=[
-            pltpu.VMEM((n - 1, shard, width), jnp.bfloat16),
-            pltpu.VMEM((experts, rows // experts, depth), jnp.bfloat16),
-            pltpu.SemaphoreType.DMA((n - 1, lanes)),
-            pltpu.SemaphoreType.DMA((n - 1, lanes)),
-            pltpu.SemaphoreType.DMA((experts,)),
-            pltpu.SemaphoreType.DMA((experts,)),
+            pltpu.VMEM((rows, width), jnp.bfloat16),
+            pltpu.VMEM((n // 2, shard, width), jnp.bfloat16),
+            pltpu.VMEM((2, experts, count, depth // 2), jnp.bfloat16),
+            pltpu.SemaphoreType.DMA((2, n // 2, parts)),
+            pltpu.SemaphoreType.DMA((n // 2, parts)),
+            pltpu.SemaphoreType.DMA((2,)),
+            pltpu.SemaphoreType.DMA((2, experts)),
+            pltpu.SemaphoreType.DMA((2, experts)),
             pltpu.SemaphoreType.DMA,
         ],
         compiler_params=pltpu.CompilerParams(

time: 269 us -> 254 us (0.944)
  Pallas kernels: 255 us -> 239 us
    pallas_call x1, Pallas kernels: 126 us -> 110 us  [expert_product(): pl.pallas_call(functools.partial(product_kernel, n, experts, shard), out_...]
where the time goes in v2:
time: 254 us
  Pallas kernels  239 us (94%)
  other arithmetic  7.45 us (3%)
  local copies, waits for them, and re-layouts  3.51 us (1%)
  matrix products  2.9 us (1%)
    pallas_call x1, Pallas kernels, reduce_grad(): pl.pallas_call(functools.partial(reduce_kernel, n, experts, shard), out_s...  129 us
    pallas_call x1, Pallas kernels, expert_product(): pl.pallas_call(functools.partial(product_kernel, n, experts, shard), out_...  110 us
    convert_element_type x1, other arithmetic, body(): master_new.astype(jnp.bfloat16)  5.81 us

profile of v2, /device:TPU:0, one launch (start us, length us, event | category | flops | bytes accessed | tf_op | source)
XLA Modules:
  0.0 253.6 jit_solution(16668011238677269635)
XLA Ops:
  0.6 0.0 copy-start
  0.6 0.9 copy.22
  1.5 0.1 reshape.44
  1.7 0.2 convert_reduce_fusion
  1.9 0.1 reduce_sum.21
  2.0 0.1 copy.23
  2.1 0.7 multiply_add_fusion
  2.8 0.7 select_reduce_fusion
  3.5 2.3 reshape.45
  5.8 0.4 convolution_convert_fusion
  6.2 0.0 copy-done
  6.2 0.0 copy-start.1
  6.2 0.0 copy-start.2
  6.3 0.0 copy-start.3
  6.3 128.7 %reduce_grad.1 = (f32[512,1536]{1,0:T(8,128)}, bf16[4,80,1536]{2,1,0:T(8,128)(2,1)S(1)}) custom-call(bf16[384,1536]{1,0:T(8,128)(2,1)S(1)} %bitcast.33, bf16[384,4096]{1,0:T(8,128)(2,1)} %bitcast.36, bf16[4,80,1536]{2,1,0:T(8,128)(2,1)S(1)} %bitcast.32), custom_call_target="tpu_custom_call" | custom-call | flops 4831838208 | bytes 25165824 | tf_op jit(solution)/shard_map/reduce_grad/pallas_call | solution.py:145
  135.0 0.0 copy-done.1
  135.0 0.0 copy-done.2
  135.0 0.0 copy-done.3
  135.0 5.8 %fusion.9 = (bf16[512,1536]{1,0:T(8,128)(2,1)S(1)}, f32[512,1536]{1,0:T(8,128)}, f32[1,512,1536]{2,1,0:T(8,128)}, f32[1,512,1536]{2,1,0:T(8,128)}) fusion(f32[512,1536]{1,0:T(8,128)} %get-tuple-element.6, f32[1,512,1536]{2,1,0:T(8,128)S(1)} %copy-done.1, f32[1,512,1536]{2,1,0:T(8,128)S(1)} %copy-done.2, f32[1,512,1536]{2,1,0:T(8,128)S(1)} %copy-done.3), kind=kLoop, calls=%fused_computation.22 | loop fusion | flops 11010048 | bytes 23592960 | tf_op jit(solution)/shard_map/convert_element_type | solution.py:379
  140.8 110.3 %expert_product.1 = bf16[4,80,4096]{2,1,0:T(8,128)(2,1)S(1)} custom-call(bf16[512,1536]{1,0:T(8,128)(2,1)S(1)} %get-tuple-element.8.weight_ref, bf16[320,1536]{1,0:T(8,128)(2,1)S(1)} %bitcast.34), custom_call_target="tpu_custom_call" | custom-call | flops 4026531840 | bytes 25165824 | tf_op jit(solution)/shard_map/expert_product/pallas_call | solution.py:334
  251.1 0.7 fusion.7
  251.9 1.7 fusion
  (1 shorter events, 0.0 us)
Async XLA Ops:
  0.6 5.6 %copy-start = (bf16[1,384,1536]{2,1,0:T(8,128)(2,1)S(1)}, bf16[1,384,1536]{2,1,0:T(8,128)(2,1)}, u32[]{:S(2)}) copy-start(bf16[1,384,1536]{2,1,0:T(8,128)(2,1)} %param.11) | copy-start | bytes 3538948
  6.2 128.8 %copy-start.1 = (f32[1,512,1536]{2,1,0:T(8,128)S(1)}, f32[1,512,1536]{2,1,0:T(8,128)}, u32[]{:S(2)}) copy-start(f32[1,512,1536]{2,1,0:T(8,128)} %param.10) | copy-start | bytes 9437188
  6.2 128.8 %copy-start.2 = (f32[1,512,1536]{2,1,0:T(8,128)S(1)}, f32[1,512,1536]{2,1,0:T(8,128)}, u32[]{:S(2)}) copy-start(f32[1,512,1536]{2,1,0:T(8,128)} %param.9) | copy-start | bytes 9437188
  6.3 128.8 %copy-start.3 = (f32[1,512,1536]{2,1,0:T(8,128)S(1)}, f32[1,512,1536]{2,1,0:T(8,128)}, u32[]{:S(2)}) copy-start(f32[1,512,1536]{2,1,0:T(8,128)} %param.8) | copy-start | bytes 9437188

commit v3 on v2

--- a/solution.py
+++ b/solution.py
@@ -59,8 +59,8 @@
 
 def reduce_kernel(
     n, experts, shard,
-    rows_ref, grads_ref, out_ref, total_ref, got_ref,
-    first, slots, part, send_sem, recv_sem, tok_send, tok_recv, own_sem,
+    rows_ref, grads_ref, pick_ref, tok_ref, total_ref, got_ref,
+    out_ref, first, slots, part, send_sem, recv_sem, tok_send, tok_recv, own_sem,
 ):
     here = ring_place(lax.axis_index("dp"), n)
     expert = lax.axis_index("expert")
@@ -101,6 +101,11 @@
     for lane, (way, low, size) in enumerate(lanes):
         first[pl.ds(low, size)] = partial(here - way, low, size).astype(jnp.bfloat16)
         send(0, lane, first).start()
+    chosen = sum(
+        jnp.dot(pick_ref[k], tok_ref[:, k, :], preferred_element_type=jnp.float32)
+        for k in range(pick_ref.shape[0])
+    )
+    out_ref[...] = chosen.astype(jnp.bfloat16).reshape(out_ref.shape)
     for other in range(1, experts):
         token_copy(other).start()
     own = pltpu.make_async_copy(out_ref.at[expert], got_ref.at[expert], own_sem)
@@ -137,20 +142,22 @@
     own.wait()
 
 
-def reduce_grad(n, experts, rows, grads, outgoing):
+def reduce_grad(n, experts, rows, grads, pick, tokens):
     saved, width = rows.shape
     depth = grads.shape[1]
     shard = depth // n
     lanes = len(lanes_of(shard))
+    queue = (experts, pick.shape[1] // experts, width)
     return pl.pallas_call(
         functools.partial(reduce_kernel, n, experts, shard),
         out_shape=(
             jax.ShapeDtypeStruct((shard, width), jnp.float32),
-            jax.ShapeDtypeStruct(outgoing.shape, jnp.bfloat16),
-        ),
-        in_specs=[pl.BlockSpec(memory_space=pltpu.VMEM)] * 3,
+            jax.ShapeDtypeStruct(queue, jnp.bfloat16),
+        ),
+        in_specs=[pl.BlockSpec(memory_space=pltpu.VMEM)] * 4,
         out_specs=(pl.BlockSpec(memory_space=pltpu.VMEM),) * 2,
         scratch_shapes=[
+            pltpu.VMEM(queue, jnp.bfloat16),
             pltpu.VMEM((shard, width), jnp.bfloat16),
             pltpu.VMEM((n - 1, shard, width), jnp.bfloat16),
             pltpu.VMEM((shard, width), jnp.float32),
@@ -167,7 +174,7 @@
             flops=2 * saved * width * depth, bytes_accessed=4 * depth * width, transcendentals=0
         ),
         name="reduce_grad",
-    )(rows, grads, outgoing)
+    )(rows, grads, pick, tokens)
 
 
 def product_kernel(
@@ -367,18 +374,13 @@
     same = (flat[:, None] == flat[None, :]) & (turn[None, :] < turn[:, None])
     slot = flat * capacity + jnp.sum(same.astype(jnp.int32), axis=1)
     places = jnp.arange(experts * capacity, dtype=jnp.int32)
-    pick = (places[:, None] == slot[None, :]).astype(jnp.bfloat16)
-    outgoing = (
-        jnp.dot(pick, slot_rows.reshape(-1, width), preferred_element_type=jnp.float32)
-        .astype(jnp.bfloat16)
-        .reshape(experts, capacity, width)
-    )
-    grad, received = reduce_grad(n, experts, saved_rows[0], saved_grads[0], outgoing)
+    slot = slot.reshape(tok_count, top_count)
+    pick = (places[None, :, None] == slot.T[:, None, :]).astype(jnp.bfloat16)
+    grad, received = reduce_grad(n, experts, saved_rows[0], saved_grads[0], pick, slot_rows)
     master_new, m_new, v_new = adam_update(master[0], moment_one[0], moment_two[0], grad)
     returned = expert_product(
         n, experts, master_new.astype(jnp.bfloat16), received.reshape(-1, width)
     ).reshape(experts * capacity, -1)
-    slot = slot.reshape(tok_count, top_count)
     share = jnp.sum(
         jnp.where(slot[:, :, None] == places[None, None, :], gates[:, :, None], 0.0), axis=1
     )

time: 254 us -> 253 us (level)
  no operation moved by 1% of the time
where the time goes in v3:
time: 253 us
  Pallas kernels  239 us (94%)
  other arithmetic  7.48 us (3%)
  local copies, waits for them, and re-layouts  3.54 us (1%)
    pallas_call x1, Pallas kernels, reduce_grad(): pl.pallas_call(functools.partial(reduce_kernel, n, experts, shard), out_s...  129 us
    pallas_call x1, Pallas kernels, expert_product(): pl.pallas_call(functools.partial(product_kernel, n, experts, shard), out_...  110 us
    convert_element_type x1, other arithmetic, body(): master_new.astype(jnp.bfloat16)  5.81 us

profile of v3, /device:TPU:0, one launch (start us, length us, event | category | flops | bytes accessed | tf_op | source)
XLA Modules:
  0.0 253.2 jit_solution(4742950062733189378)
XLA Ops:
  0.6 0.8 copy.24
  1.4 0.1 eq.42
  1.6 0.2 convert_reduce_fusion
  1.7 0.1 reduce_sum.21
  1.9 0.1 copy.25
  2.0 0.7 multiply_add_fusion
  2.7 0.7 select_reduce_fusion
  3.4 0.0 copy-start
  3.5 1.3 copy-done
  4.7 0.0 copy-start.1
  4.7 1.1 copy-done.1
  5.9 0.0 copy-start.2
  5.9 0.0 copy-start.3
  5.9 0.0 copy-start.4
  5.9 128.7 %reduce_grad.1 = (f32[512,1536]{1,0:T(8,128)}, bf16[4,80,1536]{2,1,0:T(8,128)(2,1)S(1)}) custom-call(bf16[384,1536]{1,0:T(8,128)(2,1)S(1)} %bitcast.31, bf16[384,4096]{1,0:T(8,128)(2,1)} %bitcast.35, bf16[2,320,128]{2,1,0:T(8,128)(2,1)S(1)} %fusion.4.pick_ref, bf16[128,2,1536]{2,1,0:T(2,128)(2,1)S(1)} %copy-done.1), custom_call_target="tpu_custom_call" | custom-call | flops 4831838208 | bytes 25165824 | tf_op jit(solution)/shard_map/reduce_grad/pallas_call | solution.py:151
  134.6 0.0 copy-done.2
  134.6 0.0 copy-done.3
  134.6 0.0 copy-done.4
  134.6 5.8 %fusion.9 = (bf16[512,1536]{1,0:T(8,128)(2,1)S(1)}, f32[512,1536]{1,0:T(8,128)}, f32[1,512,1536]{2,1,0:T(8,128)}, f32[1,512,1536]{2,1,0:T(8,128)}) fusion(f32[512,1536]{1,0:T(8,128)} %get-tuple-element.6, f32[1,512,1536]{2,1,0:T(8,128)S(1)} %copy-done.2, f32[1,512,1536]{2,1,0:T(8,128)S(1)} %copy-done.3, f32[1,512,1536]{2,1,0:T(8,128)S(1)} %copy-done.4), kind=kLoop, calls=%fused_computation.20 | loop fusion | flops 11010048 | bytes 23592960 | tf_op jit(solution)/shard_map/convert_element_type | solution.py:382
  140.4 110.3 %expert_product.1 = bf16[4,80,4096]{2,1,0:T(8,128)(2,1)S(1)} custom-call(bf16[512,1536]{1,0:T(8,128)(2,1)S(1)} %get-tuple-element.8.weight_ref, bf16[320,1536]{1,0:T(8,128)(2,1)S(1)} %bitcast.32), custom_call_target="tpu_custom_call" | custom-call | flops 4026531840 | bytes 25165824 | tf_op jit(solution)/shard_map/expert_product/pallas_call | solution.py:341
  250.7 0.7 fusion.7
  251.4 1.7 fusion
  (1 shorter events, 0.0 us)
Async XLA Ops:
  3.4 1.3 copy-start
  4.7 1.1 copy-start.1
  5.9 128.7 %copy-start.2 = (f32[1,512,1536]{2,1,0:T(8,128)S(1)}, f32[1,512,1536]{2,1,0:T(8,128)}, u32[]{:S(2)}) copy-start(f32[1,512,1536]{2,1,0:T(8,128)} %param.10) | copy-start | bytes 9437188
  5.9 128.7 %copy-start.3 = (f32[1,512,1536]{2,1,0:T(8,128)S(1)}, f32[1,512,1536]{2,1,0:T(8,128)}, u32[]{:S(2)}) copy-start(f32[1,512,1536]{2,1,0:T(8,128)} %param.9) | copy-start | bytes 9437188
  5.9 128.7 %copy-start.4 = (f32[1,512,1536]{2,1,0:T(8,128)S(1)}, f32[1,512,1536]{2,1,0:T(8,128)}, u32[]{:S(2)}) copy-start(f32[1,512,1536]{2,1,0:T(8,128)} %param.8) | copy-start | bytes 9437188
